TPU v7x, 32 devices: a whole 2x2x4 slice. The times are simulated.
32 devices in a mesh: parts: 2 (over y), horiz: 4 (over z), depth: 2 (over x), comp: 2 (over core).
Axes of the slice: x: 2, y: 2, z: 4, core: 2. Of those that a mesh axis runs over, the one named last changes fastest.
Arguments:
- co2_sat: float32 [1024], P(('parts', 'horiz', 'depth')), parts along dimension 0, may hold values from 0 to 0.8
- pore_press: float32 [1024], P(('parts', 'horiz', 'depth')), parts along dimension 0, may hold values from 0.5 to 1.5
- porosity: float32 [1024], P(('parts', 'horiz', 'depth')), parts along dimension 0, may hold values from 0.05 to 0.3
- facies: int32 [1024], P(('parts', 'horiz', 'depth')), parts along dimension 0, may hold values from 0 to 7
- destination: int32 [1024], P(('parts', 'horiz', 'depth')), parts along dimension 0, may hold values from 0 to 7, as said below
- mineral_mod: float32 [8], replicated, may hold values from 20 to 70
- dry_frac: float32 [8], replicated, may hold values from 0.2 to 0.6
- grain_dens: float32 [8], replicated, may hold values from 2.5 to 2.9
- relax_gain: float32 [8], replicated, may hold values from 0.1 to 0.6
- intersection_item: int32 [4, 32, 32, 128], P(None, ('parts', 'depth'), 'horiz'), parts along dimension 1, may hold values from 0 to 127, as said below
- intersection_weight: float32 [4, 32, 32, 128], P(None, ('parts', 'depth'), 'horiz'), parts along dimension 1, may hold values from 0.1 to 1
- wave_state: float32 [2, 3, 32, 32, 128], P('comp', None, ('parts', 'depth'), 'horiz'), parts along dimension 2, may hold values from -6 to 6
Outputs:
- wave_out: float32 [2, 3, 32, 32, 128], P('comp', None, ('parts', 'depth'), 'horiz'), parts along dimension 2
There are 2 independent parts, one for each index of `parts`. A program takes and returns all parts, laid end to end along the dimension named above; an argument that names none is the same for every part. Nothing has to cross between parts.
Inputs may be any that keep to these rules, and one draw needn't show every extreme that they name: `destination`: each owner's block of 64 cells names every brick at most 16 times. `intersection_item`: every entry s * 16 + j names a reservoir cell of owner s whose destination is the brick of that seismic cell and whose slot_rank is j.
All inputs are finite; a program needn't handle non-finite values.
Results may differ from a plain program's by a relative error of at most 0.0003.
Values sent between devices are 32-bit elements; how exact they have to be, the bound alone decides.
A program may use at most 64 MiB of HBM per device.

v0:
```python
import jax
import jax.numpy as jnp
from jax import lax
from jax.sharding import PartitionSpec as P

STEPS = 4
CAP = 16


coef_near = 9.0 / 8.0
coef_far = 1.0 / 24.0
courant = 0.08
brine_modulus = 2.5
brine_density = 1.03
gas_density = 0.7
gas_base = 0.02
gas_slope = 0.1
decay_fast = 0.5
decay_slow = 0.9


def shifted_2(x, axis, by):
    size = lax.axis_size(axis)
    pairs = [(i, i + by) for i in range(size) if 0 <= i + by < size]
    return lax.ppermute(x, axis, pairs)


def extended(x, sides, width):
    for axis, dim in sides:
        size, length = (lax.axis_size(axis), x.shape[dim])
        up = [(i, (i + 1) % size) for i in range(size - 1)]
        down = [(j, i) for i, j in up]
        last = lax.slice_in_dim(x, length - width, length, axis=dim)
        initial = lax.slice_in_dim(x, 0, width, axis=dim)
        before = lax.ppermute(last, axis, up)
        after = lax.ppermute(initial, axis, down)
        x = jnp.concatenate([before, x, after], axis=dim)
    return x


def shifted(values_in, along_dim, first_index, offset, count_cells):
    return lax.slice_in_dim(
        values_in, first_index + offset, first_index + offset + count_cells, axis=along_dim
    )


def forward_diff(values_in, along_dim, first_index, count_cells):
    near_part = shifted(values_in, along_dim, first_index, 1, count_cells) - shifted(
        values_in, along_dim, first_index, 0, count_cells
    )
    far_part = shifted(values_in, along_dim, first_index, 2, count_cells) - shifted(
        values_in, along_dim, first_index, -1, count_cells
    )
    return coef_near * near_part - coef_far * far_part


def backward_diff(values_in, along_dim, first_index, count_cells):
    near_part = shifted(values_in, along_dim, first_index, 0, count_cells) - shifted(
        values_in, along_dim, first_index, -1, count_cells
    )
    far_part = shifted(values_in, along_dim, first_index, 1, count_cells) - shifted(
        values_in, along_dim, first_index, -2, count_cells
    )
    return coef_near * near_part - coef_far * far_part


def rock_moduli(saturation, pressure_in, porous, k_min, dry_part, grain_rho, cell_gain):
    water_share = 1.0 - saturation
    k_gas = gas_base + gas_slope * pressure_in
    k_fluid = (brine_modulus - k_gas) * (water_share * water_share * water_share) + k_gas
    k_dry = dry_part * k_min * (1.0 - porous)
    dry_ratio = 1.0 - k_dry / k_min
    denominator = porous / k_fluid + (1.0 - porous) / k_min - k_dry / (k_min * k_min)
    k_sat = k_dry + dry_ratio * dry_ratio / denominator
    density = (1.0 - porous) * grain_rho + porous * (
        brine_density * water_share + gas_density * saturation
    )
    return jnp.stack([k_sat, density, cell_gain])


def facies_lookup(table_rows, facies_row):
    matches = (
        facies_row[None, :] == jnp.arange(table_rows.shape[0], dtype=jnp.int32)[:, None]
    ).astype(jnp.float32)
    return jnp.sum(table_rows[:, None] * matches, axis=0)


def pad_y(values_in):
    return jnp.pad(values_in, ((0, 0), (0, 0), (2, 2)))


def pressure_arrival(state_rows):
    return shifted_2(state_rows[0], "comp", -1)


def pressure_update(state_rows, divergence, bulk_modulus, memory_gain):
    arrived = shifted_2(divergence, "comp", 1)
    change = courant * bulk_modulus * arrived
    memory_fast = decay_fast * state_rows[1] + (1.0 - decay_fast) * memory_gain * change
    memory_slow = decay_slow * state_rows[2] + (1.0 - decay_slow) * memory_gain * change
    pressure = state_rows[0] - change + memory_fast + memory_slow
    return jnp.stack([pressure, memory_fast, memory_slow])


def per_device(
    co2_sat,
    pore_press,
    porosity,
    facies,
    destination,
    mineral_mod,
    dry_frac,
    grain_dens,
    relax_gain,
    intersection_item,
    intersection_weight,
    wave_state,
):
    bricks = lax.axis_size(("horiz", "depth"))
    core_index = lax.axis_index("comp")
    matches = (destination[:, None] == jnp.arange(bricks, dtype=jnp.int32)[None, :]).astype(
        jnp.int32
    )
    before = jnp.cumsum(matches, axis=0) - matches
    send_slot = destination * CAP + jnp.sum(before * matches, axis=1)
    k_min = facies_lookup(mineral_mod, facies)
    dry_part = facies_lookup(dry_frac, facies)
    grain_rho = facies_lookup(grain_dens, facies)
    cell_gain = facies_lookup(relax_gain, facies)
    raw_rows = jnp.stack([co2_sat, pore_press, porosity, k_min, dry_part, grain_rho, cell_gain])
    outgoing = jnp.ones((7, bricks * CAP), jnp.float32).at[:, send_slot].set(raw_rows)
    incoming = lax.all_to_all(outgoing, ("horiz", "depth"), split_axis=1, concat_axis=1, tiled=True)
    item_table = rock_moduli(
        incoming[0], incoming[1], incoming[2], incoming[3], incoming[4], incoming[5], incoming[6]
    )
    width_z, width_x, width_y = (
        intersection_item.shape[1],
        intersection_item.shape[2],
        intersection_item.shape[3],
    )
    summed = jnp.zeros((3, width_z, width_x, width_y), jnp.float32)
    weight_sum = jnp.zeros((width_z, width_x, width_y), jnp.float32)
    for entry in range(4):
        picked = jnp.take(item_table, intersection_item[entry], axis=1)
        summed = summed + intersection_weight[entry] * picked
        weight_sum = weight_sum + intersection_weight[entry]
    cell_props = summed / weight_sum
    bulk_modulus, density, memory_gain = (cell_props[0], cell_props[1], cell_props[2])
    fields = wave_state[0]
    for step_index in range(STEPS):
        pressure = pressure_arrival(fields)
        padded = pad_y(extended(pressure, (("horiz", 1), ("depth", 0)), 2))
        gradient = jnp.stack(
            [
                forward_diff(padded[:, 2 : 2 + width_x, 2 : 2 + width_y], 0, 2, width_z),
                forward_diff(padded[2 : 2 + width_z, :, 2 : 2 + width_y], 1, 2, width_x),
                forward_diff(padded[2 : 2 + width_z, 2 : 2 + width_x, :], 2, 2, width_y),
            ]
        )
        velocity = fields - courant * gradient / density
        vertical = extended(velocity[0], (("depth", 0),), 2)
        lateral = extended(velocity[1], (("horiz", 1),), 2)
        divergence = (
            backward_diff(vertical, 0, 2, width_z)
            + backward_diff(lateral, 1, 2, width_x)
            + backward_diff(pad_y(velocity[2]), 2, 2, width_y)
        )
        fields = jnp.where(
            core_index == 0,
            velocity,
            pressure_update(fields, divergence, bulk_modulus, memory_gain),
        )
    return fields[None]


def solution(mesh):
    in_specs = (
        P(("parts", "horiz", "depth")),
        P(("parts", "horiz", "depth")),
        P(("parts", "horiz", "depth")),
        P(("parts", "horiz", "depth")),
        P(("parts", "horiz", "depth")),
        P(),
        P(),
        P(),
        P(),
        P(None, ("parts", "depth"), "horiz", None),
        P(None, ("parts", "depth"), "horiz", None),
        P("comp", None, ("parts", "depth"), "horiz", None),
    )
    out_specs = P("comp", None, ("parts", "depth"), "horiz", None)
    return jax.shard_map(
        per_device, mesh=mesh, in_specs=in_specs, out_specs=out_specs, check_vma=False
    )
```

profile of v0, /device:TPU:0, one launch (start us, length us, event | category | flops | bytes accessed | tf_op | source)
XLA Modules:
  0.0 285.7 jit_solution(5232447901126298503)
XLA Ops:
  5.4 7.3 %all-to-all-start = ((f32[7,8,16]{2,0,1:T(8,128)}), f32[7,8,16]{2,0,1:T(8,128)S(1)}, u32[]{:S(2)}, u32[]{:S(2)}) async-start(f32[7,8,16]{2,0,1:T(8,128)} %copy.48), calls=%async_computation | async-start | bytes 65536 | tf_op jit(solution)/shard_map/all_to_all | solution.py:132
  20.3 27.7 %gather_fusion = f32[8192,3]{1,0:T(8,128)} fusion(f32[3,128]{0,1:T(8,128)S(1)} %copy.49, s32[8192]{0:T(1024)S(1)} %get-tuple-element.39), kind=kCustom, calls=%fused_computation.clone | custom fusion | bytes 229376 | tf_op jit(solution)/shard_map/jit(_take)/gather | solution.py:144
  50.8 27.7 %gather_fusion.1 = f32[8192,3]{1,0:T(8,128)} fusion(f32[3,128]{0,1:T(8,128)S(1)} %copy.49, s32[8192]{0:T(1024)S(1)} %get-tuple-element.40), kind=kCustom, calls=%fused_computation.1.clone | custom fusion | bytes 229376 | tf_op jit(solution)/shard_map/jit(_take)/gather | solution.py:144
  81.4 27.7 %gather_fusion.2 = f32[8192,3]{1,0:T(8,128)} fusion(f32[3,128]{0,1:T(8,128)S(1)} %copy.49, s32[8192]{0:T(1024)S(1)} %get-tuple-element.42), kind=kCustom, calls=%fused_computation.2.clone | custom fusion | bytes 229376 | tf_op jit(solution)/shard_map/jit(_take)/gather | solution.py:144
  112.0 27.7 %gather_fusion.3 = f32[8192,3]{1,0:T(8,128)} fusion(f32[3,128]{0,1:T(8,128)S(1)} %copy.49, s32[8192]{0:T(1024)S(1)} %get-tuple-element.41), kind=kCustom, calls=%fused_computation.3.clone | custom fusion | bytes 229376 | tf_op jit(solution)/shard_map/jit(_take)/gather | solution.py:144
  143.9 4.5 %collective-permute-start.1 = (f32[8,2,128]{2,1,0:T(2,128)S(1)}, f32[8,2,128]{2,1,0:T(2,128)S(1)}, u32[]{:S(2)}, u32[]{:S(2)}) collective-permute-start(f32[8,2,128]{2,1,0:T(2,128)S(1)} %get-tuple-element.101), channel_id=1, source_target_pairs={{0,4},{4,8},{8,12},{1,5},{5,9},{9,13},{2,6},{6,10},{10,14},{3,7},{... | collective-permute-start | bytes 24584 | tf_op jit(solution)/shard_map/ppermute | solution.py:35
  151.1 4.5 %collective-permute-start.4 = (f32[2,12,128]{2,1,0:T(8,128)S(1)}, f32[2,12,128]{2,1,0:T(8,128)S(1)}, u32[]{:S(2)}, u32[]{:S(2)}) collective-permute-start(f32[2,12,128]{2,1,0:T(8,128)S(1)} %get-tuple-element.69), channel_id=1, source_target_pairs={{0,2},{1,3},{4,6},{5,7},{8,10},{9,11},{12,14},{13,15},{16,18},{17,... | collective-permute-start | bytes 36872 | tf_op jit(solution)/shard_map/ppermute | solution.py:35
  163.0 4.2 %collective-permute-start.5 = (f32[2,8,128]{2,1,0:T(8,128)S(1)}, f32[2,8,128]{2,1,0:T(8,128)S(1)}, u32[]{:S(2)}, u32[]{:S(2)}) collective-permute-start(f32[2,8,128]{2,1,0:T(8,128)S(1)} %get-tuple-element.59), channel_id=1, source_target_pairs={{0,2},{1,3},{4,6},{5,7},{8,10},{9,11},{12,14},{13,15},{16,18},{17,... | collective-permute-start | bytes 24584 | tf_op jit(solution)/shard_map/ppermute | solution.py:35
  168.5 4.2 %collective-permute-done.6 = f32[2,8,128]{2,1,0:T(8,128)S(1)} collective-permute-done((f32[2,8,128]{2,1,0:T(8,128)S(1)}, f32[2,8,128]{2,1,0:T(8,128)S(1)}, u32[]{:S(2)}, u32[]{:S(2)}) %collective-permute-start.6) | collective-permute-done | bytes 8224 | tf_op jit(solution)/shard_map/ppermute | solution.py:36
  178.1 4.5 %collective-permute-start.11 = (f32[8,2,128]{2,1,0:T(2,128)S(1)}, f32[8,2,128]{2,1,0:T(2,128)S(1)}, u32[]{:S(2)}, u32[]{:S(2)}) collective-permute-start(f32[8,2,128]{2,1,0:T(2,128)S(1)} %get-tuple-element.95), channel_id=1, source_target_pairs={{0,4},{4,8},{8,12},{1,5},{5,9},{9,13},{2,6},{6,10},{10,14},{3,7},{... | collective-permute-start | bytes 24584 | tf_op jit(solution)/shard_map/ppermute | solution.py:35
  184.0 4.2 %collective-permute-done.12 = f32[8,2,128]{2,1,0:T(2,128)S(1)} collective-permute-done((f32[8,2,128]{2,1,0:T(2,128)S(1)}, f32[8,2,128]{2,1,0:T(2,128)S(1)}, u32[]{:S(2)}, u32[]{:S(2)}) %collective-permute-start.12) | collective-permute-done | bytes 8224 | tf_op jit(solution)/shard_map/ppermute | solution.py:36
  189.5 4.5 %collective-permute-start.14 = (f32[2,12,128]{2,1,0:T(8,128)S(1)}, f32[2,12,128]{2,1,0:T(8,128)S(1)}, u32[]{:S(2)}, u32[]{:S(2)}) collective-permute-start(f32[2,12,128]{2,1,0:T(8,128)S(1)} %get-tuple-element.67), channel_id=1, source_target_pairs={{0,2},{1,3},{4,6},{5,7},{8,10},{9,11},{12,14},{13,15},{16,18},{17,... | collective-permute-start | bytes 36872 | tf_op jit(solution)/shard_map/ppermute | solution.py:35
  199.5 4.2 %collective-permute-start.15 = (f32[2,8,128]{2,1,0:T(8,128)S(1)}, f32[2,8,128]{2,1,0:T(8,128)S(1)}, u32[]{:S(2)}, u32[]{:S(2)}) collective-permute-start(f32[2,8,128]{2,1,0:T(8,128)S(1)} %get-tuple-element.54), channel_id=1, source_target_pairs={{0,2},{1,3},{4,6},{5,7},{8,10},{9,11},{12,14},{13,15},{16,18},{17,... | collective-permute-start | bytes 24584 | tf_op jit(solution)/shard_map/ppermute | solution.py:35
  205.1 4.2 %collective-permute-done.16 = f32[2,8,128]{2,1,0:T(8,128)S(1)} collective-permute-done((f32[2,8,128]{2,1,0:T(8,128)S(1)}, f32[2,8,128]{2,1,0:T(8,128)S(1)}, u32[]{:S(2)}, u32[]{:S(2)}) %collective-permute-start.16) | collective-permute-done | bytes 8224 | tf_op jit(solution)/shard_map/ppermute | solution.py:36
  214.7 4.5 %collective-permute-start.21 = (f32[8,2,128]{2,1,0:T(2,128)S(1)}, f32[8,2,128]{2,1,0:T(2,128)S(1)}, u32[]{:S(2)}, u32[]{:S(2)}) collective-permute-start(f32[8,2,128]{2,1,0:T(2,128)S(1)} %get-tuple-element.89), channel_id=1, source_target_pairs={{0,4},{4,8},{8,12},{1,5},{5,9},{9,13},{2,6},{6,10},{10,14},{3,7},{... | collective-permute-start | bytes 24584 | tf_op jit(solution)/shard_map/ppermute | solution.py:35
  220.6 4.2 %collective-permute-done.22 = f32[8,2,128]{2,1,0:T(2,128)S(1)} collective-permute-done((f32[8,2,128]{2,1,0:T(2,128)S(1)}, f32[8,2,128]{2,1,0:T(2,128)S(1)}, u32[]{:S(2)}, u32[]{:S(2)}) %collective-permute-start.22) | collective-permute-done | bytes 8224 | tf_op jit(solution)/shard_map/ppermute | solution.py:36
  226.1 4.5 %collective-permute-start.24 = (f32[2,12,128]{2,1,0:T(8,128)S(1)}, f32[2,12,128]{2,1,0:T(8,128)S(1)}, u32[]{:S(2)}, u32[]{:S(2)}) collective-permute-start(f32[2,12,128]{2,1,0:T(8,128)S(1)} %get-tuple-element.65), channel_id=1, source_target_pairs={{0,2},{1,3},{4,6},{5,7},{8,10},{9,11},{12,14},{13,15},{16,18},{17,... | collective-permute-start | bytes 36872 | tf_op jit(solution)/shard_map/ppermute | solution.py:35
  236.7 4.2 %collective-permute-start.25 = (f32[2,8,128]{2,1,0:T(8,128)S(1)}, f32[2,8,128]{2,1,0:T(8,128)S(1)}, u32[]{:S(2)}, u32[]{:S(2)}) collective-permute-start(f32[2,8,128]{2,1,0:T(8,128)S(1)} %get-tuple-element.49), channel_id=1, source_target_pairs={{0,2},{1,3},{4,6},{5,7},{8,10},{9,11},{12,14},{13,15},{16,18},{17,... | collective-permute-start | bytes 24584 | tf_op jit(solution)/shard_map/ppermute | solution.py:35
  242.3 4.2 %collective-permute-done.26 = f32[2,8,128]{2,1,0:T(8,128)S(1)} collective-permute-done((f32[2,8,128]{2,1,0:T(8,128)S(1)}, f32[2,8,128]{2,1,0:T(8,128)S(1)}, u32[]{:S(2)}, u32[]{:S(2)}) %collective-permute-start.26) | collective-permute-done | bytes 8224 | tf_op jit(solution)/shard_map/ppermute | solution.py:36
  251.9 4.5 %collective-permute-start.31 = (f32[8,2,128]{2,1,0:T(2,128)S(1)}, f32[8,2,128]{2,1,0:T(2,128)S(1)}, u32[]{:S(2)}, u32[]{:S(2)}) collective-permute-start(f32[8,2,128]{2,1,0:T(2,128)S(1)} %get-tuple-element.83), channel_id=1, source_target_pairs={{0,4},{4,8},{8,12},{1,5},{5,9},{9,13},{2,6},{6,10},{10,14},{3,7},{... | collective-permute-start | bytes 24584 | tf_op jit(solution)/shard_map/ppermute | solution.py:35
  257.8 4.2 %collective-permute-done.32 = f32[8,2,128]{2,1,0:T(2,128)S(1)} collective-permute-done((f32[8,2,128]{2,1,0:T(2,128)S(1)}, f32[8,2,128]{2,1,0:T(2,128)S(1)}, u32[]{:S(2)}, u32[]{:S(2)}) %collective-permute-start.32) | collective-permute-done | bytes 8224 | tf_op jit(solution)/shard_map/ppermute | solution.py:36
  263.3 4.5 %collective-permute-start.34 = (f32[2,12,128]{2,1,0:T(8,128)S(1)}, f32[2,12,128]{2,1,0:T(8,128)S(1)}, u32[]{:S(2)}, u32[]{:S(2)}) collective-permute-start(f32[2,12,128]{2,1,0:T(8,128)S(1)} %get-tuple-element.63), channel_id=1, source_target_pairs={{0,2},{1,3},{4,6},{5,7},{8,10},{9,11},{12,14},{13,15},{16,18},{17,... | collective-permute-start | bytes 36872 | tf_op jit(solution)/shard_map/ppermute | solution.py:35
  273.0 4.2 %collective-permute-start.35 = (f32[2,8,128]{2,1,0:T(8,128)S(1)}, f32[2,8,128]{2,1,0:T(8,128)S(1)}, u32[]{:S(2)}, u32[]{:S(2)}) collective-permute-start(f32[2,8,128]{2,1,0:T(8,128)S(1)} %get-tuple-element.44), channel_id=1, source_target_pairs={{0,2},{1,3},{4,6},{5,7},{8,10},{9,11},{12,14},{13,15},{16,18},{17,... | collective-permute-start | bytes 24584 | tf_op jit(solution)/shard_map/ppermute | solution.py:35
  278.5 4.2 %collective-permute-done.36 = f32[2,8,128]{2,1,0:T(8,128)S(1)} collective-permute-done((f32[2,8,128]{2,1,0:T(8,128)S(1)}, f32[2,8,128]{2,1,0:T(8,128)S(1)}, u32[]{:S(2)}, u32[]{:S(2)}) %collective-permute-start.36) | collective-permute-done | bytes 8224 | tf_op jit(solution)/shard_map/ppermute | solution.py:36
  (150 shorter events, 84.3 us)
Async XLA Ops:
  5.4 13.9 %all-to-all-start = ((f32[7,8,16]{2,0,1:T(8,128)}), f32[7,8,16]{2,0,1:T(8,128)S(1)}, u32[]{:S(2)}, u32[]{:S(2)}) async-start(f32[7,8,16]{2,0,1:T(8,128)} %copy.48), calls=%async_computation | async-start | bytes 65536 | tf_op jit(solution)/shard_map/all_to_all | solution.py:132
  13.5 129.1 %collective-permute-start = (f32[8,8,128]{2,1,0:T(8,128)S(1)}, f32[8,8,128]{2,1,0:T(8,128)S(1)}, u32[]{:S(2)}, u32[]{:S(2)}) collective-permute-start(f32[8,8,128]{2,1,0:T(8,128)S(1)} %slice_bitcast_fusion.16), channel_id=1, source_target_pairs={{1,0},{3,2},{5,4},{7,6},{9,8},{11,10},{13,12},{15,14},{17,16},{19,... | collective-permute-start | bytes 98312 | tf_op jit(solution)/shard_map/ppermute | solution.py:25
  142.6 5.9 %collective-permute-start.2 = (f32[8,2,128]{2,1,0:T(2,128)S(1)}, f32[8,2,128]{2,1,0:T(2,128)S(1)}, u32[]{:S(2)}, u32[]{:S(2)}) collective-permute-start(f32[8,2,128]{2,1,0:T(2,128)S(1)} %get-tuple-element.102), channel_id=1, source_target_pairs={{4,0},{8,4},{12,8},{5,1},{9,5},{13,9},{6,2},{10,6},{14,10},{7,3},{... | collective-permute-start | bytes 24584 | tf_op jit(solution)/shard_map/ppermute | solution.py:36
  143.9 5.9 %collective-permute-start.1 = (f32[8,2,128]{2,1,0:T(2,128)S(1)}, f32[8,2,128]{2,1,0:T(2,128)S(1)}, u32[]{:S(2)}, u32[]{:S(2)}) collective-permute-start(f32[8,2,128]{2,1,0:T(2,128)S(1)} %get-tuple-element.101), channel_id=1, source_target_pairs={{0,4},{4,8},{8,12},{1,5},{5,9},{9,13},{2,6},{6,10},{10,14},{3,7},{... | collective-permute-start | bytes 24584 | tf_op jit(solution)/shard_map/ppermute | solution.py:35
  149.8 5.9 %collective-permute-start.3 = (f32[2,12,128]{2,1,0:T(8,128)S(1)}, f32[2,12,128]{2,1,0:T(8,128)S(1)}, u32[]{:S(2)}, u32[]{:S(2)}) collective-permute-start(f32[2,12,128]{2,1,0:T(8,128)S(1)} %get-tuple-element.70), channel_id=1, source_target_pairs={{2,0},{3,1},{6,4},{7,5},{10,8},{11,9},{14,12},{15,13},{18,16},{19,... | collective-permute-start | bytes 36872 | tf_op jit(solution)/shard_map/ppermute | solution.py:36
  151.1 6.0 %collective-permute-start.4 = (f32[2,12,128]{2,1,0:T(8,128)S(1)}, f32[2,12,128]{2,1,0:T(8,128)S(1)}, u32[]{:S(2)}, u32[]{:S(2)}) collective-permute-start(f32[2,12,128]{2,1,0:T(8,128)S(1)} %get-tuple-element.69), channel_id=1, source_target_pairs={{0,2},{1,3},{4,6},{5,7},{8,10},{9,11},{12,14},{13,15},{16,18},{17,... | collective-permute-start | bytes 36872 | tf_op jit(solution)/shard_map/ppermute | solution.py:35
  157.5 11.0 %collective-permute-start.7 = (f32[8,2,128]{2,1,0:T(2,128)S(1)}, f32[8,2,128]{2,1,0:T(2,128)S(1)}, u32[]{:S(2)}, u32[]{:S(2)}) collective-permute-start(f32[8,2,128]{2,1,0:T(2,128)S(1)} %get-tuple-element.98), channel_id=1, source_target_pairs={{0,4},{4,8},{8,12},{1,5},{5,9},{9,13},{2,6},{6,10},{10,14},{3,7},{... | collective-permute-start | bytes 24584 | tf_op jit(solution)/shard_map/ppermute | solution.py:35
  161.7 6.8 %collective-permute-start.8 = (f32[8,2,128]{2,1,0:T(2,128)S(1)}, f32[8,2,128]{2,1,0:T(2,128)S(1)}, u32[]{:S(2)}, u32[]{:S(2)}) collective-permute-start(f32[8,2,128]{2,1,0:T(2,128)S(1)} %get-tuple-element.97), channel_id=1, source_target_pairs={{4,0},{8,4},{12,8},{5,1},{9,5},{13,9},{6,2},{10,6},{14,10},{7,3},{... | collective-permute-start | bytes 24584 | tf_op jit(solution)/shard_map/ppermute | solution.py:36
  163.0 5.6 %collective-permute-start.5 = (f32[2,8,128]{2,1,0:T(8,128)S(1)}, f32[2,8,128]{2,1,0:T(8,128)S(1)}, u32[]{:S(2)}, u32[]{:S(2)}) collective-permute-start(f32[2,8,128]{2,1,0:T(8,128)S(1)} %get-tuple-element.59), channel_id=1, source_target_pairs={{0,2},{1,3},{4,6},{5,7},{8,10},{9,11},{12,14},{13,15},{16,18},{17,... | collective-permute-start | bytes 24584 | tf_op jit(solution)/shard_map/ppermute | solution.py:35
  178.1 5.9 %collective-permute-start.11 = (f32[8,2,128]{2,1,0:T(2,128)S(1)}, f32[8,2,128]{2,1,0:T(2,128)S(1)}, u32[]{:S(2)}, u32[]{:S(2)}) collective-permute-start(f32[8,2,128]{2,1,0:T(2,128)S(1)} %get-tuple-element.95), channel_id=1, source_target_pairs={{0,4},{4,8},{8,12},{1,5},{5,9},{9,13},{2,6},{6,10},{10,14},{3,7},{... | collective-permute-start | bytes 24584 | tf_op jit(solution)/shard_map/ppermute | solution.py:35
  188.2 5.9 %collective-permute-start.13 = (f32[2,12,128]{2,1,0:T(8,128)S(1)}, f32[2,12,128]{2,1,0:T(8,128)S(1)}, u32[]{:S(2)}, u32[]{:S(2)}) collective-permute-start(f32[2,12,128]{2,1,0:T(8,128)S(1)} %get-tuple-element.68), channel_id=1, source_target_pairs={{2,0},{3,1},{6,4},{7,5},{10,8},{11,9},{14,12},{15,13},{18,16},{19,... | collective-permute-start | bytes 36872 | tf_op jit(solution)/shard_map/ppermute | solution.py:36
  189.5 6.0 %collective-permute-start.14 = (f32[2,12,128]{2,1,0:T(8,128)S(1)}, f32[2,12,128]{2,1,0:T(8,128)S(1)}, u32[]{:S(2)}, u32[]{:S(2)}) collective-permute-start(f32[2,12,128]{2,1,0:T(8,128)S(1)} %get-tuple-element.67), channel_id=1, source_target_pairs={{0,2},{1,3},{4,6},{5,7},{8,10},{9,11},{12,14},{13,15},{16,18},{17,... | collective-permute-start | bytes 36872 | tf_op jit(solution)/shard_map/ppermute | solution.py:35
  195.9 9.1 %collective-permute-start.17 = (f32[8,2,128]{2,1,0:T(2,128)S(1)}, f32[8,2,128]{2,1,0:T(2,128)S(1)}, u32[]{:S(2)}, u32[]{:S(2)}) collective-permute-start(f32[8,2,128]{2,1,0:T(2,128)S(1)} %get-tuple-element.92), channel_id=1, source_target_pairs={{0,4},{4,8},{8,12},{1,5},{5,9},{9,13},{2,6},{6,10},{10,14},{3,7},{... | collective-permute-start | bytes 24584 | tf_op jit(solution)/shard_map/ppermute | solution.py:35
  198.2 6.8 %collective-permute-start.18 = (f32[8,2,128]{2,1,0:T(2,128)S(1)}, f32[8,2,128]{2,1,0:T(2,128)S(1)}, u32[]{:S(2)}, u32[]{:S(2)}) collective-permute-start(f32[8,2,128]{2,1,0:T(2,128)S(1)} %get-tuple-element.91), channel_id=1, source_target_pairs={{4,0},{8,4},{12,8},{5,1},{9,5},{13,9},{6,2},{10,6},{14,10},{7,3},{... | collective-permute-start | bytes 24584 | tf_op jit(solution)/shard_map/ppermute | solution.py:36
  214.7 5.9 %collective-permute-start.21 = (f32[8,2,128]{2,1,0:T(2,128)S(1)}, f32[8,2,128]{2,1,0:T(2,128)S(1)}, u32[]{:S(2)}, u32[]{:S(2)}) collective-permute-start(f32[8,2,128]{2,1,0:T(2,128)S(1)} %get-tuple-element.89), channel_id=1, source_target_pairs={{0,4},{4,8},{8,12},{1,5},{5,9},{9,13},{2,6},{6,10},{10,14},{3,7},{... | collective-permute-start | bytes 24584 | tf_op jit(solution)/shard_map/ppermute | solution.py:35
  224.8 5.9 %collective-permute-start.23 = (f32[2,12,128]{2,1,0:T(8,128)S(1)}, f32[2,12,128]{2,1,0:T(8,128)S(1)}, u32[]{:S(2)}, u32[]{:S(2)}) collective-permute-start(f32[2,12,128]{2,1,0:T(8,128)S(1)} %get-tuple-element.66), channel_id=1, source_target_pairs={{2,0},{3,1},{6,4},{7,5},{10,8},{11,9},{14,12},{15,13},{18,16},{19,... | collective-permute-start | bytes 36872 | tf_op jit(solution)/shard_map/ppermute | solution.py:36
  226.1 6.0 %collective-permute-start.24 = (f32[2,12,128]{2,1,0:T(8,128)S(1)}, f32[2,12,128]{2,1,0:T(8,128)S(1)}, u32[]{:S(2)}, u32[]{:S(2)}) collective-permute-start(f32[2,12,128]{2,1,0:T(8,128)S(1)} %get-tuple-element.65), channel_id=1, source_target_pairs={{0,2},{1,3},{4,6},{5,7},{8,10},{9,11},{12,14},{13,15},{16,18},{17,... | collective-permute-start | bytes 36872 | tf_op jit(solution)/shard_map/ppermute | solution.py:35
  232.5 9.7 %collective-permute-start.27 = (f32[8,2,128]{2,1,0:T(2,128)S(1)}, f32[8,2,128]{2,1,0:T(2,128)S(1)}, u32[]{:S(2)}, u32[]{:S(2)}) collective-permute-start(f32[8,2,128]{2,1,0:T(2,128)S(1)} %get-tuple-element.86), channel_id=1, source_target_pairs={{0,4},{4,8},{8,12},{1,5},{5,9},{9,13},{2,6},{6,10},{10,14},{3,7},{... | collective-permute-start | bytes 24584 | tf_op jit(solution)/shard_map/ppermute | solution.py:35
  235.4 6.8 %collective-permute-start.28 = (f32[8,2,128]{2,1,0:T(2,128)S(1)}, f32[8,2,128]{2,1,0:T(2,128)S(1)}, u32[]{:S(2)}, u32[]{:S(2)}) collective-permute-start(f32[8,2,128]{2,1,0:T(2,128)S(1)} %get-tuple-element.85), channel_id=1, source_target_pairs={{4,0},{8,4},{12,8},{5,1},{9,5},{13,9},{6,2},{10,6},{14,10},{7,3},{... | collective-permute-start | bytes 24584 | tf_op jit(solution)/shard_map/ppermute | solution.py:36
  251.9 5.9 %collective-permute-start.31 = (f32[8,2,128]{2,1,0:T(2,128)S(1)}, f32[8,2,128]{2,1,0:T(2,128)S(1)}, u32[]{:S(2)}, u32[]{:S(2)}) collective-permute-start(f32[8,2,128]{2,1,0:T(2,128)S(1)} %get-tuple-element.83), channel_id=1, source_target_pairs={{0,4},{4,8},{8,12},{1,5},{5,9},{9,13},{2,6},{6,10},{10,14},{3,7},{... | collective-permute-start | bytes 24584 | tf_op jit(solution)/shard_map/ppermute | solution.py:35
  262.0 5.9 %collective-permute-start.33 = (f32[2,12,128]{2,1,0:T(8,128)S(1)}, f32[2,12,128]{2,1,0:T(8,128)S(1)}, u32[]{:S(2)}, u32[]{:S(2)}) collective-permute-start(f32[2,12,128]{2,1,0:T(8,128)S(1)} %get-tuple-element.64), channel_id=1, source_target_pairs={{2,0},{3,1},{6,4},{7,5},{10,8},{11,9},{14,12},{15,13},{18,16},{19,... | collective-permute-start | bytes 36872 | tf_op jit(solution)/shard_map/ppermute | solution.py:36
  263.3 6.0 %collective-permute-start.34 = (f32[2,12,128]{2,1,0:T(8,128)S(1)}, f32[2,12,128]{2,1,0:T(8,128)S(1)}, u32[]{:S(2)}, u32[]{:S(2)}) collective-permute-start(f32[2,12,128]{2,1,0:T(8,128)S(1)} %get-tuple-element.63), channel_id=1, source_target_pairs={{0,2},{1,3},{4,6},{5,7},{8,10},{9,11},{12,14},{13,15},{16,18},{17,... | collective-permute-start | bytes 36872 | tf_op jit(solution)/shard_map/ppermute | solution.py:35
  269.8 8.7 %collective-permute-start.37 = (f32[8,2,128]{2,1,0:T(2,128)S(1)}, f32[8,2,128]{2,1,0:T(2,128)S(1)}, u32[]{:S(2)}, u32[]{:S(2)}) collective-permute-start(f32[8,2,128]{2,1,0:T(2,128)S(1)} %get-tuple-element.80), channel_id=1, source_target_pairs={{0,4},{4,8},{8,12},{1,5},{5,9},{9,13},{2,6},{6,10},{10,14},{3,7},{... | collective-permute-start | bytes 24584 | tf_op jit(solution)/shard_map/ppermute | solution.py:35
  271.7 6.8 %collective-permute-start.38 = (f32[8,2,128]{2,1,0:T(2,128)S(1)}, f32[8,2,128]{2,1,0:T(2,128)S(1)}, u32[]{:S(2)}, u32[]{:S(2)}) collective-permute-start(f32[8,2,128]{2,1,0:T(2,128)S(1)} %get-tuple-element.79), channel_id=1, source_target_pairs={{4,0},{8,4},{12,8},{5,1},{9,5},{13,9},{6,2},{10,6},{14,10},{7,3},{... | collective-permute-start | bytes 24584 | tf_op jit(solution)/shard_map/ppermute | solution.py:36
  (18 other events, 118.7 us)
where the time goes:
time: 287 us; the launch traced here: 286 us
  local copies, waits for them, and re-layouts  126 us (44%)
  starting transfers between devices  103 us (36%)
  waiting for transfers between devices  47.4 us (17%)
  other arithmetic  8.55 us (3%)
    gather x8, local copies, waits for them, and re-layouts, per_device(): picked = jnp.take(item_table, intersection_item[entry], axis=1)  122 us
    ppermute x16, starting transfers between devices, extended(): before = lax.ppermute(last, axis, up)  64.5 us
    ppermute x16, waiting for transfers between devices, extended(): after = lax.ppermute(initial, axis, down)  29.4 us
    ppermute x16, starting transfers between devices, extended(): after = lax.ppermute(initial, axis, down)  20.7 us
    ppermute x8, starting transfers between devices, shifted_2(): return lax.ppermute(x, axis, pairs)  10.3 us
    ppermute x8, waiting for transfers between devices, shifted_2(): return lax.ppermute(x, axis, pairs)  8.76 us
    all_to_all x1, starting transfers between devices, per_device(): lax.all_to_all(outgoing, ('horiz', 'depth'), split_axis=1, concat_axis=1,...  7.25 us
    ppermute x16, waiting for transfers between devices, extended(): before = lax.ppermute(last, axis, up)  7.19 us
  transfers between devices with their start and end apart: 41, of which 20 were waited for; matrix products, arithmetic and copies ran while one was open for 44% of the time, Pallas kernels for 0%

commit v1 on v0

v1 whole, which is shorter than its diff:
```python
import functools

import jax
import jax.numpy as jnp
from jax import lax
from jax.experimental import pallas as pl
from jax.experimental.pallas import tpu as pltpu
from jax.sharding import PartitionSpec as P

STEPS = 4
CAP = 16
LANES = 128
MESH = pl.DeviceIdType.MESH

coef_near = 9.0 / 8.0
coef_far = 1.0 / 24.0
courant = 0.08
brine_modulus = 2.5
brine_density = 1.03
gas_density = 0.7
gas_base = 0.02
gas_slope = 0.1
decay_fast = 0.5
decay_slow = 0.9

SIDES = (("depth", -1), ("depth", 1), ("horiz", -1), ("horiz", 1))
P_LAYERS = 3
V_LAYERS = (1, 2, 1, 2)
MESSAGES = 2 + STEPS - 1


def rock_moduli(saturation, pressure_in, porous, k_min, dry_part, grain_rho):
    water_share = 1.0 - saturation
    k_gas = gas_base + gas_slope * pressure_in
    k_fluid = (brine_modulus - k_gas) * (water_share * water_share * water_share) + k_gas
    k_dry = dry_part * k_min * (1.0 - porous)
    dry_ratio = 1.0 - k_dry / k_min
    denominator = porous / k_fluid + (1.0 - porous) / k_min - k_dry / (k_min * k_min)
    k_sat = k_dry + dry_ratio * dry_ratio / denominator
    density = (1.0 - porous) * grain_rho + porous * (
        brine_density * water_share + gas_density * saturation
    )
    return k_sat, density


def kernel(
    sat_hbm,
    press_hbm,
    poro_hbm,
    facies_hbm,
    dest_hbm,
    mineral_hbm,
    dry_hbm,
    grain_hbm,
    relax_hbm,
    item_hbm,
    weight_hbm,
    state_hbm,
    out_ref,
    cells_f,
    cells_i,
    tables,
    item,
    weight,
    own,
    other,
    table_send,
    table_recv,
    z_send,
    x_send,
    z_recv,
    x_recv,
    p_x,
    v_x,
    rd_x,
    local_sem,
    partner_sem,
    table_send_sem,
    table_recv_sem,
    side_send_sem,
    side_recv_sem,
):
    horiz, depth, comp = (lax.axis_index(a) for a in ("horiz", "depth", "comp"))
    n_horiz, n_depth = lax.axis_size("horiz"), lax.axis_size("depth")
    bricks = n_horiz * n_depth
    me = horiz * n_depth + depth
    cells = dest_hbm.shape[1]
    facies_count = mineral_hbm.shape[0]
    nz, nx, ny = item.shape[1:]
    chunks = table_send.shape[0]
    here = {"depth": depth, "horiz": horiz}
    extent = {"depth": n_depth, "horiz": n_horiz}

    barrier = pltpu.get_barrier_semaphore()

    def brick_id(q):
        return {"horiz": q // n_depth, "depth": lax.rem(q, n_depth)}

    partner = {"comp": 1 - comp}

    z_recv[...] = jnp.zeros_like(z_recv)
    x_recv[...] = jnp.zeros_like(x_recv)

    def each_brick(body):
        if bricks <= 16:
            for d in range(1, bricks):
                body(d)
        else:
            lax.fori_loop(1, bricks, lambda d, c: (body(d), c)[1], 0)

    def greet(d):
        pl.semaphore_signal(
            barrier, inc=1, device_id=brick_id(lax.rem(me + d, bricks)), device_id_type=MESH
        )

    each_brick(greet)
    pl.semaphore_signal(barrier, inc=1, device_id=partner, device_id_type=MESH)

    sources = (
        (sat_hbm, cells_f.at[0]),
        (press_hbm, cells_f.at[1]),
        (poro_hbm, cells_f.at[2]),
        (facies_hbm, cells_i.at[0]),
        (dest_hbm, cells_i.at[1]),
        (mineral_hbm, tables.at[0]),
        (dry_hbm, tables.at[1]),
        (grain_hbm, tables.at[2]),
        (relax_hbm, tables.at[3]),
        (state_hbm.at[0], own),
        (item_hbm, item),
        (weight_hbm, weight),
    )
    loads = [
        pltpu.make_async_copy(src, dst, local_sem.at[k]) for k, (src, dst) in enumerate(sources)
    ]
    for load in loads:
        load.start()
    for load in loads[:9]:
        load.wait()

    facies = cells_i[0]
    drow = cells_i[1]
    picked = []
    for t in range(4):
        row = jnp.zeros(facies.shape, jnp.float32)
        for k in range(facies_count):
            row = jnp.where(facies == k, tables[t, k], row)
        picked.append(row)
    k_sat, rho = rock_moduli(cells_f[0], cells_f[1], cells_f[2], *picked[:3])
    row_id = lax.broadcasted_iota(jnp.int32, (8, cells), 0)
    moduli = jnp.where(
        row_id == 0, k_sat, jnp.where(row_id == 1, rho, jnp.where(row_id == 2, picked[3], 0.0))
    )
    high = moduli.astype(jnp.bfloat16)
    rest = moduli - high.astype(jnp.float32)
    middle = rest.astype(jnp.bfloat16)
    low = (rest - middle.astype(jnp.float32)).astype(jnp.bfloat16)
    pieces = jnp.concatenate(
        [high.astype(jnp.float32), middle.astype(jnp.float32), low.astype(jnp.float32)], axis=0
    ).astype(jnp.bfloat16)
    width = bricks * CAP
    group = min(cells, LANES)
    placed = jnp.zeros((24, width), jnp.float32)
    for first in range(0, cells, group):
        down = lax.broadcasted_iota(jnp.int32, (group, cells), 0) + first
        along = lax.broadcasted_iota(jnp.int32, (group, cells), 1)
        drow_f = drow.astype(jnp.float32)
        spread = jnp.broadcast_to(drow_f, (group, cells))
        dcol = jnp.sum(jnp.where(down == along, spread, 0.0), axis=1, keepdims=True)
        rank = jnp.sum(
            jnp.where((spread == dcol) & (along < down), 1.0, 0.0), axis=1, keepdims=True
        )
        slot = dcol * CAP + rank
        target = lax.broadcasted_iota(jnp.int32, (group, width), 1).astype(jnp.float32)
        place = jnp.where(slot == target, 1.0, 0.0).astype(jnp.bfloat16)
        placed = placed + jnp.dot(
            pieces[:, first : first + group], place, preferred_element_type=jnp.float32
        )
    table = placed[0:8] + placed[8:16] + placed[16:24]
    for c in range(chunks):
        table_send[c] = table[:, c * LANES : (c + 1) * LANES]

    pl.semaphore_wait(barrier, bricks)

    def table_copy(d):
        return pltpu.make_async_remote_copy(
            src_ref=table_send,
            dst_ref=table_recv.at[me],
            send_sem=table_send_sem.at[d],
            recv_sem=table_recv_sem.at[d],
            device_id=brick_id(lax.rem(me + d, bricks)),
            device_id_type=MESH,
        )

    each_brick(lambda d: table_copy(d).start())
    loads[9].wait()
    swap = pltpu.make_async_remote_copy(
        src_ref=own,
        dst_ref=other,
        send_sem=partner_sem.at[0],
        recv_sem=partner_sem.at[1],
        device_id=partner,
        device_id_type=MESH,
    )
    swap.start()
    table_recv[me] = table_send[...]

    def side_copy(message, side, rows):
        axis, step = SIDES[side]
        send, recv = (z_send, z_recv) if axis == "depth" else (x_send, x_recv)
        mine, theirs = side % 2, (side % 2) ^ 1
        return pltpu.make_async_remote_copy(
            src_ref=send.at[message, mine, pl.ds(0, rows)],
            dst_ref=recv.at[message, theirs, pl.ds(0, rows)],
            send_sem=side_send_sem.at[message, side],
            recv_sem=side_recv_sem.at[message, side ^ 1],
            device_id={axis: here[axis] + step},
            device_id_type=MESH,
        )

    def rows_of(message, side):
        if message == 0:
            return P_LAYERS + V_LAYERS[side]
        return V_LAYERS[side] if message == 1 else P_LAYERS

    def exists(side):
        axis, step = SIDES[side]
        place = here[axis] + step
        return (place >= 0) & (place < extent[axis])

    def start_sides(message):
        for side in range(4):

            @pl.when(exists(side))
            def _(side=side):
                side_copy(message, side, rows_of(message, side)).start()

    def wait_sides(message):
        for side in range(4):

            @pl.when(exists(side))
            def _(side=side):
                side_copy(message, side ^ 1, rows_of(message, side ^ 1)).wait_recv()

    def wait_sent(message):
        for side in range(4):

            @pl.when(exists(side))
            def _(side=side):
                side_copy(message, side, rows_of(message, side)).wait_send()

    def pack(message, first, along_z, along_x, layers_low, layers_high):
        z_send[message, 0, first : first + layers_low] = along_z[0:layers_low]
        z_send[message, 1, first : first + layers_high] = along_z[nz - layers_high :]
        for k in range(layers_low):
            x_send[message, 0, first + k] = along_x[:, k, :]
        for k in range(layers_high):
            x_send[message, 1, first + k] = along_x[:, nx - layers_high + k, :]

    lane = lax.broadcasted_iota(jnp.int32, (nz, nx, ny), 2)

    def moved_y(f, offset):
        rolled = pltpu.roll(f, (-offset) % ny, 2)
        keep = lane < ny - offset if offset > 0 else lane >= -offset
        return jnp.where(keep, rolled, 0.0)

    def forward(f0, f1, f2, fm1):
        return coef_near * (f1 - f0) - coef_far * (f2 - fm1)

    def backward(f0, fm1, f1, fm2):
        return coef_near * (f0 - fm1) - coef_far * (f1 - fm2)

    swap.wait_recv()
    first_core = comp == 0
    velocity = [jnp.where(first_core, own[k], other[k]) for k in range(3)]
    pressure, memory_fast, memory_slow = (
        jnp.where(first_core, other[k], own[k]) for k in range(3)
    )
    pack(0, 0, pressure, pressure, P_LAYERS, P_LAYERS)
    pack(0, P_LAYERS, velocity[0], velocity[1], 1, 2)
    start_sides(0)

    each_brick(lambda d: table_copy(d).wait_recv())
    lane_row = lax.broadcasted_iota(jnp.int32, (8, LANES), 1)
    per = LANES // CAP
    my_chunk, my_lane = me // per, lax.rem(me, per) * CAP
    item_rows = []
    for c in range(chunks):
        total = jnp.zeros((8, LANES), jnp.float32)
        for k in range(per):
            tile = table_recv[c * per + k, my_chunk]
            turned = pltpu.roll(tile, lax.rem(k * CAP - my_lane + LANES, LANES), 1)
            total = jnp.where((lane_row >= k * CAP) & (lane_row < (k + 1) * CAP), turned, total)
        item_rows.append(total)

    loads[10].wait()
    loads[11].wait()

    def lookup(r, index):
        found = jnp.zeros((nx, ny), jnp.float32)
        for c in range(chunks):
            source = jnp.broadcast_to(item_rows[c][r : r + 1], (nx, LANES))
            got = jnp.take_along_axis(
                source, lax.rem(index, LANES), axis=1, mode="promise_in_bounds"
            )
            found = got if chunks == 1 else jnp.where(index // LANES == c, got, found)
        return found

    def remap(r):
        return jnp.stack(
            [
                sum(weight[e, z] * lookup(r, item[e, z]) for e in range(4))
                for z in range(nz)
            ]
        )

    weight_sum = weight[0] + weight[1] + weight[2] + weight[3]
    rd = courant * weight_sum / remap(1)
    pack(1, 0, rd, rd, 1, 2)
    start_sides(1)
    bulk = courant * remap(0) / weight_sum
    gain = remap(2) / weight_sum
    gain_fast = (1.0 - decay_fast) * gain
    gain_slow = (1.0 - decay_slow) * gain

    def fill_p(message):
        for k in range(P_LAYERS):
            p_x[:, k, :] = x_recv[message, 0, k]
            p_x[:, P_LAYERS + nx + k, :] = x_recv[message, 1, k]

    span = v_x.shape[1]
    v_x[...] = jnp.zeros_like(v_x)
    rd_x[...] = jnp.zeros_like(rd_x)
    p_x[...] = jnp.zeros_like(p_x)

    wait_sides(0)
    v_x[:, 2 : 2 + nx, :] = velocity[1]
    for k in range(2):
        v_x[:, k, :] = x_recv[0, 0, P_LAYERS + k]
    v_x[:, 2 + nx, :] = x_recv[0, 1, P_LAYERS]
    vz_low, vz_high = z_recv[0, 0, P_LAYERS : P_LAYERS + 2], z_recv[0, 1, P_LAYERS : P_LAYERS + 1]
    v_z = jnp.concatenate([vz_low, velocity[0], vz_high], axis=0)
    v_y = velocity[2]
    rd_x[:, 2 : 2 + nx, :] = rd

    for step in range(STEPS):
        message = 0 if step == 0 else 1 + step
        p_x[:, P_LAYERS : P_LAYERS + nx, :] = pressure
        v_y = v_y - rd * forward(
            pressure, moved_y(pressure, 1), moved_y(pressure, 2), moved_y(pressure, -1)
        )
        part_y = backward(v_y, moved_y(v_y, -1), moved_y(v_y, 1), moved_y(v_y, -2))
        if step == 0:
            wait_sides(1)
            for k in range(2):
                rd_x[:, k, :] = x_recv[1, 0, k]
            rd_x[:, 2 + nx, :] = x_recv[1, 1, 0]
            rd_z = jnp.concatenate([z_recv[1, 0, 0:2], rd, z_recv[1, 1, 0:1]], axis=0)
        else:
            wait_sides(message)
        fill_p(message)
        p_z = jnp.concatenate(
            [z_recv[message, 0, 0:P_LAYERS], pressure, z_recv[message, 1, 0:P_LAYERS]], axis=0
        )
        n = nz + 3
        v_z = v_z - rd_z * forward(
            p_z[1 : 1 + n], p_z[2 : 2 + n], p_z[3 : 3 + n], p_z[0:n]
        )
        v_x[...] = v_x[...] - rd_x[...] * forward(
            p_x[:, 1 : 1 + span, :],
            p_x[:, 2 : 2 + span, :],
            p_x[:, 3 : 3 + span, :],
            p_x[:, 0:span, :],
        )
        part_z = backward(
            v_z[2 : 2 + nz], v_z[1 : 1 + nz], v_z[3 : 3 + nz], v_z[0:nz]
        )
        part_x = backward(
            v_x[:, 2 : 2 + nx, :],
            v_x[:, 1 : 1 + nx, :],
            v_x[:, 3 : 3 + nx, :],
            v_x[:, 0:nx, :],
        )
        change = bulk * (part_z + part_x + part_y)
        memory_fast = decay_fast * memory_fast + gain_fast * change
        memory_slow = decay_slow * memory_slow + gain_slow * change
        pressure = pressure - change + memory_fast + memory_slow
        if step < STEPS - 1:
            pack(2 + step, 0, pressure, pressure, P_LAYERS, P_LAYERS)
            start_sides(2 + step)

    out_ref[0, 0] = jnp.where(first_core, v_z[2 : 2 + nz], pressure)
    out_ref[0, 1] = jnp.where(first_core, v_x[:, 2 : 2 + nx, :], memory_fast)
    out_ref[0, 2] = jnp.where(first_core, v_y, memory_slow)

    each_brick(lambda d: table_copy(d).wait_send())
    swap.wait_send()
    for message in range(MESSAGES):
        wait_sent(message)


def per_device(
    co2_sat,
    pore_press,
    porosity,
    facies,
    destination,
    mineral_mod,
    dry_frac,
    grain_dens,
    relax_gain,
    intersection_item,
    intersection_weight,
    wave_state,
):
    bricks = lax.axis_size(("horiz", "depth"))
    cells = destination.shape[0]
    nz, nx, ny = intersection_item.shape[1:]
    chunks = bricks * CAP // LANES
    span = 8 * -(-(nx + 3) // 8)
    layers = P_LAYERS + 2
    rows = [v.reshape(1, cells) for v in (co2_sat, pore_press, porosity, facies, destination)]
    f32 = jnp.float32
    return pl.pallas_call(
        kernel,
        out_shape=jax.ShapeDtypeStruct(wave_state.shape, f32),
        in_specs=[pl.BlockSpec(memory_space=pl.ANY)] * 12,
        out_specs=pl.BlockSpec(memory_space=pltpu.VMEM),
        scratch_shapes=[
            pltpu.VMEM((3, 1, cells), f32),
            pltpu.VMEM((2, 1, cells), jnp.int32),
            pltpu.SMEM((4, mineral_mod.shape[0]), f32),
            pltpu.VMEM(intersection_item.shape, jnp.int32),
            pltpu.VMEM(intersection_weight.shape, f32),
            pltpu.VMEM((3, nz, nx, ny), f32),
            pltpu.VMEM((3, nz, nx, ny), f32),
            pltpu.VMEM((chunks, 8, LANES), f32),
            pltpu.VMEM((bricks, chunks, 8, LANES), f32),
            pltpu.VMEM((MESSAGES, 2, layers, nx, ny), f32),
            pltpu.VMEM((MESSAGES, 2, layers, nz, ny), f32),
            pltpu.VMEM((MESSAGES, 2, layers, nx, ny), f32),
            pltpu.VMEM((MESSAGES, 2, layers, nz, ny), f32),
            pltpu.VMEM((nz, span + 8, ny), f32),
            pltpu.VMEM((nz, span, ny), f32),
            pltpu.VMEM((nz, span, ny), f32),
            pltpu.SemaphoreType.DMA((12,)),
            pltpu.SemaphoreType.DMA((2,)),
            pltpu.SemaphoreType.DMA((bricks,)),
            pltpu.SemaphoreType.DMA((bricks,)),
            pltpu.SemaphoreType.DMA((MESSAGES, 4)),
            pltpu.SemaphoreType.DMA((MESSAGES, 4)),
        ],
        compiler_params=pltpu.CompilerParams(
            collective_id=0, has_side_effects=True, vmem_limit_bytes=48 * 1024 * 1024
        ),
        name="remap_and_steps",
    )(
        *rows,
        mineral_mod,
        dry_frac,
        grain_dens,
        relax_gain,
        intersection_item,
        intersection_weight,
        wave_state,
    )


def solution(mesh):
    in_specs = (
        P(("parts", "horiz", "depth")),
        P(("parts", "horiz", "depth")),
        P(("parts", "horiz", "depth")),
        P(("parts", "horiz", "depth")),
        P(("parts", "horiz", "depth")),
        P(),
        P(),
        P(),
        P(),
        P(None, ("parts", "depth"), "horiz", None),
        P(None, ("parts", "depth"), "horiz", None),
        P("comp", None, ("parts", "depth"), "horiz", None),
    )
    out_specs = P("comp", None, ("parts", "depth"), "horiz", None)
    return jax.shard_map(
        per_device, mesh=mesh, in_specs=in_specs, out_specs=out_specs, check_vma=False
    )
```

time: 287 us -> 26.7 us (0.09)
  local copies, waits for them, and re-layouts: 126 us -> 4.08 us
  starting transfers between devices: 103 us -> 0 us
  waiting for transfers between devices: 47.4 us -> 0 us
  Pallas kernels: 0 us -> 22.4 us
  other arithmetic: 8.55 us -> 0 us
    gather x8 -> x0, local copies, waits for them, and re-layouts: 122 us -> none  [per_device(): picked = jnp.take(item_table, intersection_item[entry], axis=1)]
    ppermute x40 -> x0, starting transfers between devices: 95.5 us -> none  [the longest x16 64.5 us: extended(): before = lax.ppermute(last, axis, up)]
    ppermute x40 -> x0, waiting for transfers between devices: 45.3 us -> none  [the longest x16 29.4 us: extended(): after = lax.ppermute(initial, axis, down)]
    pallas_call x0 -> x1, Pallas kernels: none -> 22.4 us  [per_device(): pl.pallas_call(kernel, out_shape=jax.ShapeDtypeStruct(wave_state.shape, f...]
    all_to_all x1 -> x0, starting transfers between devices: 7.25 us -> none  [per_device(): lax.all_to_all(outgoing, ('horiz', 'depth'), split_axis=1, concat_axis=1,...]
    unnamed x2 -> x25, local copies, waits for them, and re-layouts: 0.01 us -> 4.08 us
  transfers between devices with their start and end apart: 41 -> 0, of which waited for: 20 -> 0; matrix products, arithmetic and copies ran while one was open for 44% -> 0% of each run, Pallas kernels for 0% -> 0%
where the time goes in v1:
time: 26.7 us; the launch traced here: 26.5 us
  Pallas kernels  22.4 us (84%)
  local copies, waits for them, and re-layouts  4.08 us (15%)
    pallas_call x1, Pallas kernels, per_device(): pl.pallas_call(kernel, out_shape=jax.ShapeDtypeStruct(wave_state.shape, f...  22.4 us
    unnamed x25, local copies, waits for them, and re-layouts  4.08 us

profile of v1, /device:TPU:0, one launch (start us, length us, event | category | flops | bytes accessed | tf_op | source)
XLA Modules:
  0.0 26.5 jit_solution(2021253952176701120)
XLA Ops:
  0.0 0.0 copy-start.10
  0.0 0.0 copy-start.11
  0.0 0.0 copy-start.6
  0.0 0.0 copy-start.7
  0.0 0.0 copy-start.8
  0.0 0.0 copy-start.9
  0.0 0.0 copy-start.3
  0.0 0.0 copy-start.4
  0.0 0.0 copy-start.5
  0.1 0.6 %copy-done.10 = f32[8]{0:T(128)S(1)} copy-done((f32[8]{0:T(128)S(1)}, f32[8]{0:T(128)}, u32[]{:S(2)}) %copy-start.10) | copy-done | bytes 56
  0.7 0.0 copy-done.11
  0.7 0.0 copy-done.6
  0.7 0.0 copy-done.7
  0.7 0.0 copy-done.8
  0.7 0.0 copy-done.9
  0.7 0.0 copy-done.3
  0.8 0.0 copy-done.4
  0.8 0.0 copy-done.5
  0.8 0.0 copy-start
  0.8 0.9 %copy-done = s32[4,8,8,128]{3,2,1,0:T(8,128)S(1)} copy-done((s32[4,8,8,128]{3,2,1,0:T(8,128)S(1)}, s32[4,8,8,128]{3,2,1,0:T(8,128)}, u32[]{:S(2)}) %copy-start) | copy-done | bytes 131096
  1.7 0.9 %copy-done.1 = f32[4,8,8,128]{3,2,1,0:T(8,128)S(1)} copy-done((f32[4,8,8,128]{3,2,1,0:T(8,128)S(1)}, f32[4,8,8,128]{3,2,1,0:T(8,128)}, u32[]{:S(2)}) %copy-start.1) | copy-done | bytes 131096
  2.6 0.9 %copy-done.2 = f32[1,3,8,8,128]{4,3,2,1,0:T(8,128)S(1)} copy-done((f32[1,3,8,8,128]{4,3,2,1,0:T(8,128)S(1)}, f32[1,3,8,8,128]{4,3,2,1,0:T(8,128)}, u32[]{:S(2)}) %copy-start.2) | copy-done | bytes 98328
  3.5 22.4 %remap_and_steps.1 = f32[1,3,8,8,128]{4,3,2,1,0:T(8,128)S(1)} custom-call(f32[1,64]{1,0:T(1,128)S(1)} %bitcast.5, f32[1,64]{1,0:T(1,128)S(1)} %bitcast.6, f32[1,64]{1,0:T(1,128)S(1)} %bitcast.7, s32[1,64]{1,0:T(1,128)S(1)} %bitcast.8, s32[1,64]{1,0:T(1,128)S(1)} %bitcast.9, f32[8]{0:T(128)S(1)} %copy-done.8, f32[8]{0:T(128)S(1)} %copy-done.9, ...), custom_call_target="tpu_custom_call" | custom-call | tf_op jit(solution)/shard_map/remap_and_steps/pallas_call | solution.py:424
  25.9 0.6 %copy.14 = f32[1,3,8,8,128]{4,3,2,1,0:T(8,128)} copy(f32[1,3,8,8,128]{4,3,2,1,0:T(8,128)S(1)} %remap_and_steps.1) | data formatting | bytes 196608
  (2 shorter events, 0.0 us)
Async XLA Ops:
  0.0 0.7 %copy-start.10 = (f32[8]{0:T(128)S(1)}, f32[8]{0:T(128)}, u32[]{:S(2)}) copy-start(f32[8]{0:T(128)} %grain_hbm.1) | copy-start | bytes 100
  0.0 0.7 %copy-start.11 = (f32[8]{0:T(128)S(1)}, f32[8]{0:T(128)}, u32[]{:S(2)}) copy-start(f32[8]{0:T(128)} %relax_hbm.1) | copy-start | bytes 100
  0.0 0.7 %copy-start.6 = (s32[64]{0:T(128)S(1)}, s32[64]{0:T(128)}, u32[]{:S(2)}) copy-start(s32[64]{0:T(128)} %param.15) | copy-start | bytes 772
  0.0 0.7 %copy-start.7 = (s32[64]{0:T(128)S(1)}, s32[64]{0:T(128)}, u32[]{:S(2)}) copy-start(s32[64]{0:T(128)} %param.16) | copy-start | bytes 772
  0.0 0.7 %copy-start.8 = (f32[8]{0:T(128)S(1)}, f32[8]{0:T(128)}, u32[]{:S(2)}) copy-start(f32[8]{0:T(128)} %mineral_hbm.1) | copy-start | bytes 100
  0.0 0.7 %copy-start.9 = (f32[8]{0:T(128)S(1)}, f32[8]{0:T(128)}, u32[]{:S(2)}) copy-start(f32[8]{0:T(128)} %dry_hbm.1) | copy-start | bytes 100
  0.0 0.7 %copy-start.3 = (f32[64]{0:T(128)S(1)}, f32[64]{0:T(128)}, u32[]{:S(2)}) copy-start(f32[64]{0:T(128)} %param.12) | copy-start | bytes 772
  0.0 0.7 %copy-start.4 = (f32[64]{0:T(128)S(1)}, f32[64]{0:T(128)}, u32[]{:S(2)}) copy-start(f32[64]{0:T(128)} %param.13) | copy-start | bytes 772
  0.0 0.7 %copy-start.5 = (f32[64]{0:T(128)S(1)}, f32[64]{0:T(128)}, u32[]{:S(2)}) copy-start(f32[64]{0:T(128)} %param.14) | copy-start | bytes 772
  0.8 0.9 %copy-start = (s32[4,8,8,128]{3,2,1,0:T(8,128)S(1)}, s32[4,8,8,128]{3,2,1,0:T(8,128)}, u32[]{:S(2)}) copy-start(s32[4,8,8,128]{3,2,1,0:T(8,128)} %item_hbm.1) | copy-start | bytes 393220
  1.7 0.9 %copy-start.1 = (f32[4,8,8,128]{3,2,1,0:T(8,128)S(1)}, f32[4,8,8,128]{3,2,1,0:T(8,128)}, u32[]{:S(2)}) copy-start(f32[4,8,8,128]{3,2,1,0:T(8,128)} %weight_hbm.1) | copy-start | bytes 393220
  2.6 0.9 %copy-start.2 = (f32[1,3,8,8,128]{4,3,2,1,0:T(8,128)S(1)}, f32[1,3,8,8,128]{4,3,2,1,0:T(8,128)}, u32[]{:S(2)}) copy-start(f32[1,3,8,8,128]{4,3,2,1,0:T(8,128)} %state_hbm.1) | copy-start | bytes 294916

commit v2 on v1

--- a/solution.py
+++ b/solution.py
@@ -98,8 +98,19 @@
 
     partner = {"comp": 1 - comp}
 
-    z_recv[...] = jnp.zeros_like(z_recv)
-    x_recv[...] = jnp.zeros_like(x_recv)
+    def exists(side):
+        axis, step = SIDES[side]
+        place = here[axis] + step
+        return (place >= 0) & (place < extent[axis])
+
+    for side in range(4):
+
+        @pl.when(jnp.logical_not(exists(side)))
+        def _(side=side):
+            halo = (z_recv, x_recv)[side // 2]
+            for message in range(MESSAGES):
+                rows = halo.shape[2] if message == 1 else P_LAYERS + 2
+                halo[message, side % 2, 0:rows] = jnp.zeros((rows,) + halo.shape[3:], jnp.float32)
 
     def each_brick(body):
         if bricks <= 16:
@@ -221,12 +232,7 @@
     def rows_of(message, side):
         if message == 0:
             return P_LAYERS + V_LAYERS[side]
-        return V_LAYERS[side] if message == 1 else P_LAYERS
-
-    def exists(side):
-        axis, step = SIDES[side]
-        place = here[axis] + step
-        return (place >= 0) & (place < extent[axis])
+        return 8 * V_LAYERS[side] if message == 1 else P_LAYERS
 
     def start_sides(message):
         for side in range(4):
@@ -249,13 +255,14 @@
             def _(side=side):
                 side_copy(message, side, rows_of(message, side)).wait_send()
 
-    def pack(message, first, along_z, along_x, layers_low, layers_high):
-        z_send[message, 0, first : first + layers_low] = along_z[0:layers_low]
-        z_send[message, 1, first : first + layers_high] = along_z[nz - layers_high :]
+    def pack(message, first, along_z, along_x, layers_low, layers_high, apart=1):
         for k in range(layers_low):
-            x_send[message, 0, first + k] = along_x[:, k, :]
+            z_send[message, 0, first + apart * k] = along_z[k].astype(jnp.float32)
+            x_send[message, 0, first + apart * k] = along_x[:, k, :].astype(jnp.float32)
         for k in range(layers_high):
-            x_send[message, 1, first + k] = along_x[:, nx - layers_high + k, :]
+            layer_z, layer_x = nz - layers_high + k, nx - layers_high + k
+            z_send[message, 1, first + apart * k] = along_z[layer_z].astype(jnp.float32)
+            x_send[message, 1, first + apart * k] = along_x[:, layer_x, :].astype(jnp.float32)
 
     lane = lax.broadcasted_iota(jnp.int32, (nz, nx, ny), 2)
 
@@ -269,6 +276,13 @@
 
     def backward(f0, fm1, f1, fm2):
         return coef_near * (f0 - fm1) - coef_far * (f1 - fm2)
+
+    loads[10].wait()
+    loads[11].wait()
+    for e in range(4):
+        pack(1, 2 * e, item.at[e], item.at[e], 1, 2, 8)
+        pack(1, 2 * e + 1, weight.at[e], weight.at[e], 1, 2, 8)
+    start_sides(1)
 
     swap.wait_recv()
     first_core = comp == 0
@@ -283,45 +297,63 @@
     each_brick(lambda d: table_copy(d).wait_recv())
     lane_row = lax.broadcasted_iota(jnp.int32, (8, LANES), 1)
     per = LANES // CAP
-    my_chunk, my_lane = me // per, lax.rem(me, per) * CAP
-    item_rows = []
-    for c in range(chunks):
-        total = jnp.zeros((8, LANES), jnp.float32)
-        for k in range(per):
-            tile = table_recv[c * per + k, my_chunk]
-            turned = pltpu.roll(tile, lax.rem(k * CAP - my_lane + LANES, LANES), 1)
-            total = jnp.where((lane_row >= k * CAP) & (lane_row < (k + 1) * CAP), turned, total)
-        item_rows.append(total)
-
-    loads[10].wait()
-    loads[11].wait()
-
-    def lookup(r, index):
-        found = jnp.zeros((nx, ny), jnp.float32)
+
+    def brick_table(brick):
+        chunk, first = brick // per, lax.rem(brick, per) * CAP
+        rows = []
         for c in range(chunks):
-            source = jnp.broadcast_to(item_rows[c][r : r + 1], (nx, LANES))
+            total = jnp.zeros((8, LANES), jnp.float32)
+            for k in range(per):
+                tile = table_recv[c * per + k, chunk]
+                turned = pltpu.roll(tile, lax.rem(k * CAP - first + LANES, LANES), 1)
+                total = jnp.where(
+                    (lane_row >= k * CAP) & (lane_row < (k + 1) * CAP), turned, total
+                )
+            rows.append(total)
+        return rows
+
+    def lookup(rows, r, index):
+        found = jnp.zeros(index.shape, jnp.float32)
+        for c in range(chunks):
+            source = jnp.broadcast_to(rows[c][r : r + 1], (index.shape[0], LANES))
             got = jnp.take_along_axis(
                 source, lax.rem(index, LANES), axis=1, mode="promise_in_bounds"
             )
             found = got if chunks == 1 else jnp.where(index // LANES == c, got, found)
         return found
 
+    own_rows = brick_table(me)
+
     def remap(r):
         return jnp.stack(
             [
-                sum(weight[e, z] * lookup(r, item[e, z]) for e in range(4))
+                sum(weight[e, z] * lookup(own_rows, r, item[e, z]) for e in range(4))
                 for z in range(nz)
             ]
         )
 
     weight_sum = weight[0] + weight[1] + weight[2] + weight[3]
     rd = courant * weight_sum / remap(1)
-    pack(1, 0, rd, rd, 1, 2)
-    start_sides(1)
     bulk = courant * remap(0) / weight_sum
     gain = remap(2) / weight_sum
     gain_fast = (1.0 - decay_fast) * gain
     gain_slow = (1.0 - decay_slow) * gain
+
+    def halo_rd(side):
+        axis, step = SIDES[side]
+        recv = (z_recv, x_recv)[side // 2]
+        there = {**here, axis: jnp.where(exists(side), here[axis] + step, here[axis])}
+        rows = brick_table(there["horiz"] * n_depth + there["depth"])
+        found = []
+        for k in range(V_LAYERS[side ^ 1]):
+            total, scale = 0.0, 0.0
+            for e in range(4):
+                index = recv[1, side % 2, 8 * k + 2 * e].astype(jnp.int32)
+                share = recv[1, side % 2, 8 * k + 2 * e + 1]
+                total = total + share * lookup(rows, 1, index)
+                scale = scale + share
+            found.append(jnp.where(exists(side), courant * scale / total, 0.0))
+        return found
 
     def fill_p(message):
         for k in range(P_LAYERS):
@@ -352,10 +384,11 @@
         part_y = backward(v_y, moved_y(v_y, -1), moved_y(v_y, 1), moved_y(v_y, -2))
         if step == 0:
             wait_sides(1)
+            halos = [halo_rd(side) for side in range(4)]
             for k in range(2):
-                rd_x[:, k, :] = x_recv[1, 0, k]
-            rd_x[:, 2 + nx, :] = x_recv[1, 1, 0]
-            rd_z = jnp.concatenate([z_recv[1, 0, 0:2], rd, z_recv[1, 1, 0:1]], axis=0)
+                rd_x[:, k, :] = halos[2][k]
+            rd_x[:, 2 + nx, :] = halos[3][0]
+            rd_z = jnp.concatenate([jnp.stack(halos[0]), rd, jnp.stack(halos[1])], axis=0)
         else:
             wait_sides(message)
         fill_p(message)
@@ -418,13 +451,13 @@
     nz, nx, ny = intersection_item.shape[1:]
     chunks = bricks * CAP // LANES
     span = 8 * -(-(nx + 3) // 8)
-    layers = P_LAYERS + 2
+    layers = max(P_LAYERS + 2, 8 * max(V_LAYERS))
     rows = [v.reshape(1, cells) for v in (co2_sat, pore_press, porosity, facies, destination)]
     f32 = jnp.float32
     return pl.pallas_call(
         kernel,
         out_shape=jax.ShapeDtypeStruct(wave_state.shape, f32),
-        in_specs=[pl.BlockSpec(memory_space=pl.ANY)] * 12,
+        in_specs=[pl.BlockSpec(memory_space=pltpu.HBM)] * 12,
         out_specs=pl.BlockSpec(memory_space=pltpu.VMEM),
         scratch_shapes=[
             pltpu.VMEM((3, 1, cells), f32),
@@ -451,7 +484,7 @@
             pltpu.SemaphoreType.DMA((MESSAGES, 4)),
         ],
         compiler_params=pltpu.CompilerParams(
-            collective_id=0, has_side_effects=True, vmem_limit_bytes=48 * 1024 * 1024
+            collective_id=0, has_side_effects=True, vmem_limit_bytes=55040 * 1024
         ),
         name="remap_and_steps",
     )(

time: 26.7 us -> 21.5 us (0.81)
  local copies, waits for them, and re-layouts: 4.08 us -> 1.38 us
  Pallas kernels: 22.4 us -> 19.9 us
    unnamed x25 -> x19, local copies, waits for them, and re-layouts: 4.08 us -> 1.38 us
    pallas_call x1, Pallas kernels: 22.4 us -> 19.9 us  [per_device(): pl.pallas_call(kernel, out_shape=jax.ShapeDtypeStruct(wave_state.shape, f...]
where the time goes in v2:
time: 21.5 us; the launch traced here: 21.3 us
  Pallas kernels  19.9 us (93%)
  local copies, waits for them, and re-layouts  1.38 us (6%)
    pallas_call x1, Pallas kernels, per_device(): pl.pallas_call(kernel, out_shape=jax.ShapeDtypeStruct(wave_state.shape, f...  19.9 us
    unnamed x19, local copies, waits for them, and re-layouts  1.38 us

profile of v2, /device:TPU:0, one launch (start us, length us, event | category | flops | bytes accessed | tf_op | source)
XLA Modules:
  0.0 21.3 jit_solution(3372315790113331336)
XLA Ops:
  0.0 0.0 copy-start.7
  0.0 0.0 copy-start.8
  0.0 0.0 copy-start.3
  0.0 0.0 copy-start.4
  0.0 0.0 copy-start.5
  0.0 0.0 copy-start.6
  0.0 0.0 copy-start
  0.0 0.0 copy-start.1
  0.0 0.0 copy-start.2
  0.1 0.6 %copy-done.7 = f32[8]{0:T(128)S(1)} copy-done((f32[8]{0:T(128)S(1)}, f32[8]{0:T(128)}, u32[]{:S(2)}) %copy-start.7) | copy-done | bytes 56
  0.7 0.0 copy-done.8
  0.7 0.0 copy-done.3
  0.7 0.0 copy-done.4
  0.7 0.0 copy-done.5
  0.7 0.0 copy-done.6
  0.7 0.0 copy-done
  0.8 0.0 copy-done.1
  0.8 0.0 copy-done.2
  0.8 19.9 %remap_and_steps.1 = f32[1,3,8,8,128]{4,3,2,1,0:T(8,128)S(1)} custom-call(f32[1,64]{1,0:T(1,128)S(1)} %bitcast.5, f32[1,64]{1,0:T(1,128)S(1)} %bitcast.6, f32[1,64]{1,0:T(1,128)S(1)} %bitcast.7, s32[1,64]{1,0:T(1,128)S(1)} %bitcast.8, s32[1,64]{1,0:T(1,128)S(1)} %bitcast.9, f32[8]{0:T(128)S(1)} %copy-done.5, f32[8]{0:T(128)S(1)} %copy-done.6, ...), custom_call_target="tpu_custom_call" | custom-call | tf_op jit(solution)/shard_map/remap_and_steps/pallas_call | solution.py:457
  20.7 0.6 %copy.14 = f32[1,3,8,8,128]{4,3,2,1,0:T(8,128)} copy(f32[1,3,8,8,128]{4,3,2,1,0:T(8,128)S(1)} %remap_and_steps.1) | data formatting | bytes 196608
Async XLA Ops:
  0.0 0.7 %copy-start.7 = (f32[8]{0:T(128)S(1)}, f32[8]{0:T(128)}, u32[]{:S(2)}) copy-start(f32[8]{0:T(128)} %grain_hbm.1) | copy-start | bytes 100
  0.0 0.7 %copy-start.8 = (f32[8]{0:T(128)S(1)}, f32[8]{0:T(128)}, u32[]{:S(2)}) copy-start(f32[8]{0:T(128)} %relax_hbm.1) | copy-start | bytes 100
  0.0 0.7 %copy-start.3 = (s32[64]{0:T(128)S(1)}, s32[64]{0:T(128)}, u32[]{:S(2)}) copy-start(s32[64]{0:T(128)} %param.15) | copy-start | bytes 772
  0.0 0.7 %copy-start.4 = (s32[64]{0:T(128)S(1)}, s32[64]{0:T(128)}, u32[]{:S(2)}) copy-start(s32[64]{0:T(128)} %param.16) | copy-start | bytes 772
  0.0 0.7 %copy-start.5 = (f32[8]{0:T(128)S(1)}, f32[8]{0:T(128)}, u32[]{:S(2)}) copy-start(f32[8]{0:T(128)} %mineral_hbm.1) | copy-start | bytes 100
  0.0 0.7 %copy-start.6 = (f32[8]{0:T(128)S(1)}, f32[8]{0:T(128)}, u32[]{:S(2)}) copy-start(f32[8]{0:T(128)} %dry_hbm.1) | copy-start | bytes 100
  0.0 0.7 %copy-start = (f32[64]{0:T(128)S(1)}, f32[64]{0:T(128)}, u32[]{:S(2)}) copy-start(f32[64]{0:T(128)} %param.12) | copy-start | bytes 772
  0.0 0.7 %copy-start.1 = (f32[64]{0:T(128)S(1)}, f32[64]{0:T(128)}, u32[]{:S(2)}) copy-start(f32[64]{0:T(128)} %param.13) | copy-start | bytes 772
  0.0 0.7 %copy-start.2 = (f32[64]{0:T(128)S(1)}, f32[64]{0:T(128)}, u32[]{:S(2)}) copy-start(f32[64]{0:T(128)} %param.14) | copy-start | bytes 772

commit v3 on v2

--- a/solution.py
+++ b/solution.py
@@ -235,14 +235,14 @@
         return 8 * V_LAYERS[side] if message == 1 else P_LAYERS
 
     def start_sides(message):
-        for side in range(4):
+        for side in (2, 3, 0, 1):
 
             @pl.when(exists(side))
             def _(side=side):
                 side_copy(message, side, rows_of(message, side)).start()
 
-    def wait_sides(message):
-        for side in range(4):
+    def wait_sides(message, sides=(2, 3, 0, 1)):
+        for side in sides:
 
             @pl.when(exists(side))
             def _(side=side):
@@ -389,30 +389,32 @@
                 rd_x[:, k, :] = halos[2][k]
             rd_x[:, 2 + nx, :] = halos[3][0]
             rd_z = jnp.concatenate([jnp.stack(halos[0]), rd, jnp.stack(halos[1])], axis=0)
-        else:
-            wait_sides(message)
+        if step > 0:
+            wait_sides(message, (2, 3))
         fill_p(message)
-        p_z = jnp.concatenate(
-            [z_recv[message, 0, 0:P_LAYERS], pressure, z_recv[message, 1, 0:P_LAYERS]], axis=0
-        )
-        n = nz + 3
-        v_z = v_z - rd_z * forward(
-            p_z[1 : 1 + n], p_z[2 : 2 + n], p_z[3 : 3 + n], p_z[0:n]
-        )
         v_x[...] = v_x[...] - rd_x[...] * forward(
             p_x[:, 1 : 1 + span, :],
             p_x[:, 2 : 2 + span, :],
             p_x[:, 3 : 3 + span, :],
             p_x[:, 0:span, :],
         )
-        part_z = backward(
-            v_z[2 : 2 + nz], v_z[1 : 1 + nz], v_z[3 : 3 + nz], v_z[0:nz]
-        )
         part_x = backward(
             v_x[:, 2 : 2 + nx, :],
             v_x[:, 1 : 1 + nx, :],
             v_x[:, 3 : 3 + nx, :],
             v_x[:, 0:nx, :],
+        )
+        if step > 0:
+            wait_sides(message, (0, 1))
+        p_z = jnp.concatenate(
+            [z_recv[message, 0, 0:P_LAYERS], pressure, z_recv[message, 1, 0:P_LAYERS]], axis=0
+        )
+        n = nz + 3
+        v_z = v_z - rd_z * forward(
+            p_z[1 : 1 + n], p_z[2 : 2 + n], p_z[3 : 3 + n], p_z[0:n]
+        )
+        part_z = backward(
+            v_z[2 : 2 + nz], v_z[1 : 1 + nz], v_z[3 : 3 + nz], v_z[0:nz]
         )
         change = bulk * (part_z + part_x + part_y)
         memory_fast = decay_fast * memory_fast + gain_fast * change
@@ -421,15 +423,17 @@
         if step < STEPS - 1:
             pack(2 + step, 0, pressure, pressure, P_LAYERS, P_LAYERS)
             start_sides(2 + step)
+            if step == 0:
+                each_brick(lambda d: table_copy(d).wait_send())
+                swap.wait_send()
+                wait_sent(0)
+            wait_sent(1 + step)
 
     out_ref[0, 0] = jnp.where(first_core, v_z[2 : 2 + nz], pressure)
     out_ref[0, 1] = jnp.where(first_core, v_x[:, 2 : 2 + nx, :], memory_fast)
     out_ref[0, 2] = jnp.where(first_core, v_y, memory_slow)
 
-    each_brick(lambda d: table_copy(d).wait_send())
-    swap.wait_send()
-    for message in range(MESSAGES):
-        wait_sent(message)
+    wait_sent(MESSAGES - 1)
 
 
 def per_device(

time: 21.5 us -> 21.3 us (level)
  no operation moved by 1% of the time
where the time goes in v3:
time: 21.3 us; the launch traced here: 21.2 us
  Pallas kernels  19.7 us (92%)
  local copies, waits for them, and re-layouts  1.38 us (6%)
    pallas_call x1, Pallas kernels, per_device(): pl.pallas_call(kernel, out_shape=jax.ShapeDtypeStruct(wave_state.shape, f...  19.7 us
    unnamed x19, local copies, waits for them, and re-layouts  1.38 us

profile of v3, /device:TPU:0, one launch (start us, length us, event | category | flops | bytes accessed | tf_op | source)
XLA Modules:
  0.0 21.2 jit_solution(14597095619501603892)
XLA Ops:
  0.0 0.0 copy-start.7
  0.0 0.0 copy-start.8
  0.0 0.0 copy-start.3
  0.0 0.0 copy-start.4
  0.0 0.0 copy-start.5
  0.0 0.0 copy-start.6
  0.0 0.0 copy-start
  0.0 0.0 copy-start.1
  0.0 0.0 copy-start.2
  0.1 0.6 %copy-done.7 = f32[8]{0:T(128)S(1)} copy-done((f32[8]{0:T(128)S(1)}, f32[8]{0:T(128)}, u32[]{:S(2)}) %copy-start.7) | copy-done | bytes 56
  0.7 0.0 copy-done.8
  0.7 0.0 copy-done.3
  0.7 0.0 copy-done.4
  0.7 0.0 copy-done.5
  0.7 0.0 copy-done.6
  0.7 0.0 copy-done
  0.8 0.0 copy-done.1
  0.8 0.0 copy-done.2
  0.8 19.7 %remap_and_steps.1 = f32[1,3,8,8,128]{4,3,2,1,0:T(8,128)S(1)} custom-call(f32[1,64]{1,0:T(1,128)S(1)} %bitcast.5, f32[1,64]{1,0:T(1,128)S(1)} %bitcast.6, f32[1,64]{1,0:T(1,128)S(1)} %bitcast.7, s32[1,64]{1,0:T(1,128)S(1)} %bitcast.8, s32[1,64]{1,0:T(1,128)S(1)} %bitcast.9, f32[8]{0:T(128)S(1)} %copy-done.5, f32[8]{0:T(128)S(1)} %copy-done.6, ...), custom_call_target="tpu_custom_call" | custom-call | tf_op jit(solution)/shard_map/remap_and_steps/pallas_call | solution.py:461
  20.5 0.6 %copy.14 = f32[1,3,8,8,128]{4,3,2,1,0:T(8,128)} copy(f32[1,3,8,8,128]{4,3,2,1,0:T(8,128)S(1)} %remap_and_steps.1) | data formatting | bytes 196608
Async XLA Ops:
  0.0 0.7 %copy-start.7 = (f32[8]{0:T(128)S(1)}, f32[8]{0:T(128)}, u32[]{:S(2)}) copy-start(f32[8]{0:T(128)} %grain_hbm.1) | copy-start | bytes 100
  0.0 0.7 %copy-start.8 = (f32[8]{0:T(128)S(1)}, f32[8]{0:T(128)}, u32[]{:S(2)}) copy-start(f32[8]{0:T(128)} %relax_hbm.1) | copy-start | bytes 100
  0.0 0.7 %copy-start.3 = (s32[64]{0:T(128)S(1)}, s32[64]{0:T(128)}, u32[]{:S(2)}) copy-start(s32[64]{0:T(128)} %param.15) | copy-start | bytes 772
  0.0 0.7 %copy-start.4 = (s32[64]{0:T(128)S(1)}, s32[64]{0:T(128)}, u32[]{:S(2)}) copy-start(s32[64]{0:T(128)} %param.16) | copy-start | bytes 772
  0.0 0.7 %copy-start.5 = (f32[8]{0:T(128)S(1)}, f32[8]{0:T(128)}, u32[]{:S(2)}) copy-start(f32[8]{0:T(128)} %mineral_hbm.1) | copy-start | bytes 100
  0.0 0.7 %copy-start.6 = (f32[8]{0:T(128)S(1)}, f32[8]{0:T(128)}, u32[]{:S(2)}) copy-start(f32[8]{0:T(128)} %dry_hbm.1) | copy-start | bytes 100
  0.0 0.7 %copy-start = (f32[64]{0:T(128)S(1)}, f32[64]{0:T(128)}, u32[]{:S(2)}) copy-start(f32[64]{0:T(128)} %param.12) | copy-start | bytes 772
  0.0 0.7 %copy-start.1 = (f32[64]{0:T(128)S(1)}, f32[64]{0:T(128)}, u32[]{:S(2)}) copy-start(f32[64]{0:T(128)} %param.13) | copy-start | bytes 772
  0.0 0.7 %copy-start.2 = (f32[64]{0:T(128)S(1)}, f32[64]{0:T(128)}, u32[]{:S(2)}) copy-start(f32[64]{0:T(128)} %param.14) | copy-start | bytes 772

commit v4 on v3

--- a/solution.py
+++ b/solution.py
@@ -216,7 +216,7 @@
     swap.start()
     table_recv[me] = table_send[...]
 
-    def side_copy(message, side, rows):
+    def side_copy(message, side, rows, arriving=False):
         axis, step = SIDES[side]
         send, recv = (z_send, z_recv) if axis == "depth" else (x_send, x_recv)
         mine, theirs = side % 2, (side % 2) ^ 1
@@ -225,7 +225,7 @@
             dst_ref=recv.at[message, theirs, pl.ds(0, rows)],
             send_sem=side_send_sem.at[message, side],
             recv_sem=side_recv_sem.at[message, side ^ 1],
-            device_id={axis: here[axis] + step},
+            device_id={axis: here[axis] + (-step if arriving else step)},
             device_id_type=MESH,
         )
 
@@ -246,7 +246,7 @@
 
             @pl.when(exists(side))
             def _(side=side):
-                side_copy(message, side ^ 1, rows_of(message, side ^ 1)).wait_recv()
+                side_copy(message, side ^ 1, rows_of(message, side ^ 1), True).wait_recv()
 
     def wait_sent(message):
         for side in range(4):

time: 21.3 us -> 21.3 us (level)
  no operation moved by 1% of the time
where the time goes in v4:
time: 21.3 us; the launch traced here: 21.2 us
  Pallas kernels  19.7 us (92%)
  local copies, waits for them, and re-layouts  1.38 us (6%)
    pallas_call x1, Pallas kernels, per_device(): pl.pallas_call(kernel, out_shape=jax.ShapeDtypeStruct(wave_state.shape, f...  19.7 us
    unnamed x19, local copies, waits for them, and re-layouts  1.38 us

profile of v4, /device:TPU:0, one launch (start us, length us, event | category | flops | bytes accessed | tf_op | source)
XLA Modules:
  0.0 21.2 jit_solution(14597095619501603892)
XLA Ops:
  0.0 0.0 copy-start.7
  0.0 0.0 copy-start.8
  0.0 0.0 copy-start.3
  0.0 0.0 copy-start.4
  0.0 0.0 copy-start.5
  0.0 0.0 copy-start.6
  0.0 0.0 copy-start
  0.0 0.0 copy-start.1
  0.0 0.0 copy-start.2
  0.1 0.6 %copy-done.7 = f32[8]{0:T(128)S(1)} copy-done((f32[8]{0:T(128)S(1)}, f32[8]{0:T(128)}, u32[]{:S(2)}) %copy-start.7) | copy-done | bytes 56
  0.7 0.0 copy-done.8
  0.7 0.0 copy-done.3
  0.7 0.0 copy-done.4
  0.7 0.0 copy-done.5
  0.7 0.0 copy-done.6
  0.7 0.0 copy-done
  0.8 0.0 copy-done.1
  0.8 0.0 copy-done.2
  0.8 19.7 %remap_and_steps.1 = f32[1,3,8,8,128]{4,3,2,1,0:T(8,128)S(1)} custom-call(f32[1,64]{1,0:T(1,128)S(1)} %bitcast.5, f32[1,64]{1,0:T(1,128)S(1)} %bitcast.6, f32[1,64]{1,0:T(1,128)S(1)} %bitcast.7, s32[1,64]{1,0:T(1,128)S(1)} %bitcast.8, s32[1,64]{1,0:T(1,128)S(1)} %bitcast.9, f32[8]{0:T(128)S(1)} %copy-done.5, f32[8]{0:T(128)S(1)} %copy-done.6, ...), custom_call_target="tpu_custom_call" | custom-call | tf_op jit(solution)/shard_map/remap_and_steps/pallas_call | solution.py:461
  20.5 0.6 %copy.14 = f32[1,3,8,8,128]{4,3,2,1,0:T(8,128)} copy(f32[1,3,8,8,128]{4,3,2,1,0:T(8,128)S(1)} %remap_and_steps.1) | data formatting | bytes 196608
Async XLA Ops:
  0.0 0.7 %copy-start.7 = (f32[8]{0:T(128)S(1)}, f32[8]{0:T(128)}, u32[]{:S(2)}) copy-start(f32[8]{0:T(128)} %grain_hbm.1) | copy-start | bytes 100
  0.0 0.7 %copy-start.8 = (f32[8]{0:T(128)S(1)}, f32[8]{0:T(128)}, u32[]{:S(2)}) copy-start(f32[8]{0:T(128)} %relax_hbm.1) | copy-start | bytes 100
  0.0 0.7 %copy-start.3 = (s32[64]{0:T(128)S(1)}, s32[64]{0:T(128)}, u32[]{:S(2)}) copy-start(s32[64]{0:T(128)} %param.15) | copy-start | bytes 772
  0.0 0.7 %copy-start.4 = (s32[64]{0:T(128)S(1)}, s32[64]{0:T(128)}, u32[]{:S(2)}) copy-start(s32[64]{0:T(128)} %param.16) | copy-start | bytes 772
  0.0 0.7 %copy-start.5 = (f32[8]{0:T(128)S(1)}, f32[8]{0:T(128)}, u32[]{:S(2)}) copy-start(f32[8]{0:T(128)} %mineral_hbm.1) | copy-start | bytes 100
  0.0 0.7 %copy-start.6 = (f32[8]{0:T(128)S(1)}, f32[8]{0:T(128)}, u32[]{:S(2)}) copy-start(f32[8]{0:T(128)} %dry_hbm.1) | copy-start | bytes 100
  0.0 0.7 %copy-start = (f32[64]{0:T(128)S(1)}, f32[64]{0:T(128)}, u32[]{:S(2)}) copy-start(f32[64]{0:T(128)} %param.12) | copy-start | bytes 772
  0.0 0.7 %copy-start.1 = (f32[64]{0:T(128)S(1)}, f32[64]{0:T(128)}, u32[]{:S(2)}) copy-start(f32[64]{0:T(128)} %param.13) | copy-start | bytes 772
  0.0 0.7 %copy-start.2 = (f32[64]{0:T(128)S(1)}, f32[64]{0:T(128)}, u32[]{:S(2)}) copy-start(f32[64]{0:T(128)} %param.14) | copy-start | bytes 772
